TPU v7x, 512 devices: a whole 4x4x16 slice. The times are simulated.
512 devices in a mesh: ix: 4 (over x), iy: 8 (over y, core), depth: 16 (over z).
Axes of the slice: x: 4, y: 4, z: 16, core: 2. Of those that a mesh axis runs over, the one named last changes fastest.
Arguments:
- density: float32 [1024, 1024, 512], P('depth', 'iy', 'ix'), may hold values from -4 to 4
- color_coeffs: float32 [3, 4], replicated, may hold values from -1 to 1
- opacity_coeffs: float32 [4], replicated, may hold values from -1 to 1
- light: float32 [3], replicated, may hold values from -1 to 1
Outputs:
- image: float32 [4, 1024, 512], P(None, ('iy', 'depth'), 'ix')
All inputs are finite; a program needn't handle non-finite values.
Results may differ from a plain program's by a relative error of at most 0.0003.
Values sent between devices are 32-bit elements; how exact they have to be, the bound alone decides.
A program may use at most 64 MiB of HBM per device.

v0:
```python
import jax
import jax.numpy as jnp
from jax import lax
from jax.sharding import PartitionSpec as P


def with_halo(x, sides, width):
    for axis, dim in sides:
        size, length = (lax.axis_size(axis), x.shape[dim])
        up = [(i, (i + 1) % size) for i in range(size - 1)]
        down = [(j, i) for i, j in up]
        last = lax.slice_in_dim(x, length - width, length, axis=dim)
        first = lax.slice_in_dim(x, 0, width, axis=dim)
        before = lax.ppermute(last, axis, up)
        after = lax.ppermute(first, axis, down)
        x = jnp.concatenate([before, x, after], axis=dim)
    return x


def polynomial(coeffs, values):
    result = jnp.zeros_like(values) + coeffs[-1]
    for degree in range(coeffs.shape[0] - 2, -1, -1):
        result = result * values + coeffs[degree]
    return result


def shade_block(padded, color_coeffs, opacity_coeffs, light, depth_total):
    centre = padded[1:-1, 1:-1, 1:-1]
    grad_z = 0.5 * (padded[2:, 1:-1, 1:-1] - padded[:-2, 1:-1, 1:-1])
    grad_y = 0.5 * (padded[1:-1, 2:, 1:-1] - padded[1:-1, :-2, 1:-1])
    grad_x = 0.5 * (padded[1:-1, 1:-1, 2:] - padded[1:-1, 1:-1, :-2])
    scaled = centre * 0.25
    extinction = 3.0 / depth_total * polynomial(opacity_coeffs, scaled) ** 2
    facing = grad_x * light[0] + grad_y * light[1] + grad_z * light[2]
    shading = 0.3 + 0.7 * jnp.abs(facing) / jnp.sqrt(
        grad_x * grad_x + grad_y * grad_y + grad_z * grad_z + 1.0
    )
    before = jnp.cumsum(extinction, 0) - extinction
    weight = jnp.exp(-before) * (1.0 - jnp.exp(-extinction)) * shading
    colors = [
        jnp.sum(weight * polynomial(color_coeffs[channel], scaled) ** 2, 0) for channel in range(3)
    ]
    optical = jnp.sum(extinction, 0)
    return jnp.stack(colors + [optical])


def per_device(density, color_coeffs, opacity_coeffs, light):
    layers = lax.axis_size("depth")
    brick_z, brick_y, brick_x = density.shape
    padded = with_halo(density, (("depth", 0), ("iy", 1), ("ix", 2)), 1)
    partial_value = shade_block(
        padded, color_coeffs, opacity_coeffs, light, float(brick_z * layers)
    )
    parts = lax.all_to_all(partial_value[None], "depth", split_axis=2, concat_axis=0, tiled=True)
    optical = parts[:, 3]
    before = jnp.cumsum(optical, 0) - optical
    colors = jnp.sum(jnp.exp(-before)[:, None] * parts[:, :3], 0)
    total = jnp.sum(optical, 0)
    return jnp.concatenate([colors, jnp.exp(-total)[None]], 0)


def solution(mesh):
    return jax.shard_map(
        per_device,
        mesh=mesh,
        in_specs=(P("depth", "iy", "ix"), P(), P(), P()),
        out_specs=P(None, ("iy", "depth"), "ix"),
        check_vma=False,
    )
```

profile of v0, /device:TPU:1, one launch (start us, length us, event | category | flops | bytes accessed | tf_op | source)
XLA Modules:
  0.0 146.1 jit_solution(8047254173668555196)
XLA Ops:
  0.0 0.9 fusion.24
  0.9 4.4 %collective-permute-start = (f32[1,128,128]{2,1,0:T(8,128)S(1)}, f32[1,128,128]{2,1,0:T(8,128)S(1)}, u32[]{:S(2)}, u32[]{:S(2)}) collective-permute-start(f32[1,128,128]{2,1,0:T(8,128)S(1)} %get-tuple-element.14), channel_id=1, source_target_pairs={{0,1},{1,2},{2,3},{3,4},{4,5},{5,6},{6,7},{7,8},{8,9},{9,10},{10,1... | collective-permute-start | bytes 196616 | tf_op jit(solution)/shard_map/ppermute | solution.py:14
  5.3 1.3 collective-permute-start.1
  6.6 1.8 %fusion.25 = (f32[1,1]{1,0:T(1,128)}, f32[1,1]{1,0:T(1,128)}, f32[1,1]{1,0:T(1,128)}, f32[1,1]{1,0:T(1,128)}, f32[1,1]{1,0:T(1,128)}, /*index=5*/f32[1,1]{1,0:T(...) fusion(f32[3,4]{1,0:T(4,128)} %param.5), kind=kLoop, calls=%fused_computation.52 | loop fusion | bytes 96 | tf_op jit(solution)/shard_map/slice | solution.py:21
  8.3 0.0 collective-permute-done
  8.4 0.0 copy-start.1
  8.4 2.7 %constant_dynamic-update-slice_fusion.1 = f32[66,128,128]{2,1,0:T(8,128)S(1)} fusion(f32[66,128,128]{2,1,0:T(8,128)S(1)} %constant_dynamic-update-slice_fusion.2, f32[64,128,128]{2,1,0:T(8,128)} %param.4), kind=kLoop, calls=%fused_computation.44 | loop fusion | bytes 8388608
  11.1 0.0 collective-permute-done.1
  11.1 0.0 copy-start
  11.2 4.4 %collective-permute-start.2 = (f32[66,1,128]{2,1,0:T(1,128)S(1)}, f32[66,1,128]{2,1,0:T(1,128)S(1)}, u32[]{:S(2)}, u32[]{:S(2)}) collective-permute-start(f32[66,1,128]{2,1,0:T(1,128)S(1)} %get-tuple-element.12), channel_id=1, source_target_pairs={{0,16},{16,32},{32,48},{48,64},{64,80},{80,96},{96,112},{1,17},{17... | collective-permute-start | bytes 101384 | tf_op jit(solution)/shard_map/ppermute | solution.py:14
  15.5 3.0 %collective-permute-start.3 = (f32[66,1,128]{2,1,0:T(1,128)S(1)}, f32[66,1,128]{2,1,0:T(1,128)S(1)}, u32[]{:S(2)}, u32[]{:S(2)}) collective-permute-start(f32[66,1,128]{2,1,0:T(1,128)S(1)} %get-tuple-element.11), channel_id=1, source_target_pairs={{16,0},{32,16},{48,32},{64,48},{80,64},{96,80},{112,96},{17,1},{33... | collective-permute-start | bytes 101384 | tf_op jit(solution)/shard_map/ppermute | solution.py:15
  18.5 0.0 copy-done.1
  18.5 0.7 fusion.27
  19.2 0.0 collective-permute-done.2
  19.2 1.6 %collective-permute-done.3 = f32[66,1,128]{2,1,0:T(1,128)S(1)} collective-permute-done((f32[66,1,128]{2,1,0:T(1,128)S(1)}, f32[66,1,128]{2,1,0:T(1,128)S(1)}, u32[]{:S(2)}, u32[]{:S(2)}) %collective-permute-start.3) | collective-permute-done | bytes 33824 | tf_op jit(solution)/shard_map/ppermute | solution.py:15
  20.8 0.0 copy-done
  20.8 0.7 pad_maximum_fusion
  21.5 4.9 %fusion.22 = (f32[66,130,1]{2,1,0:T(8,128)}, f32[66,130,1]{2,1,0:T(8,128)}) fusion(f32[66,130,128]{2,1,0:T(8,128)S(1)} %pad_maximum_fusion), kind=kLoop, calls=%fused_computation.49 | loop fusion | bytes 137280 | tf_op jit(solution)/shard_map/slice | solution.py:13
  26.4 0.0 copy-start.2
  26.4 3.6 %copy.6 = f32[66,130,1]{0,2,1:T(1,128)S(1)} copy(f32[66,130,1]{2,1,0:T(8,128)} %get-tuple-element.9) | data formatting | bytes 68640 | tf_op jit(solution)/shard_map/slice | solution.py:13
  30.0 1.3 collective-permute-start.4
  31.3 3.6 %copy.8 = f32[66,130,1]{0,2,1:T(1,128)S(1)} copy(f32[66,130,1]{2,1,0:T(8,128)} %get-tuple-element.10) | data formatting | bytes 68640 | tf_op jit(solution)/shard_map/slice | solution.py:12
  34.9 4.0 %collective-permute-start.5 = (f32[66,130,1]{0,2,1:T(1,128)S(1)}, f32[66,130,1]{0,2,1:T(1,128)S(1)}, u32[]{:S(2)}, u32[]{:S(2)}) collective-permute-start(f32[66,130,1]{0,2,1:T(1,128)S(1)} %copy.8), channel_id=1, source_target_pairs={{0,128},{128,256},{256,384},{1,129},{129,257},{257,385},{2,130},{1... | collective-permute-start | bytes 102968 | tf_op jit(solution)/shard_map/ppermute | solution.py:14
  38.9 0.0 copy-done.2
  38.9 0.7 fusion.26
  44.0 0.0 collective-permute-done.4
  44.0 3.4 %copy.7 = f32[66,130,1]{2,1,0:T(8,128)} copy(f32[66,130,1]{0,2,1:T(1,128)S(1)} %collective-permute-done.4) | data formatting | bytes 68640 | tf_op jit(solution)/shard_map/ppermute | solution.py:15
  47.4 0.0 collective-permute-done.5
  47.4 3.4 %copy.9 = f32[66,130,1]{2,1,0:T(8,128)} copy(f32[66,130,1]{0,2,1:T(1,128)S(1)} %collective-permute-done.5) | data formatting | bytes 68640 | tf_op jit(solution)/shard_map/ppermute | solution.py:14
  50.8 60.8 %fusion.11 = (f32[128,128]{1,0:T(8,128)S(1)}, f32[128,128]{1,0:T(8,128)S(1)}, f32[128,128]{1,0:T(8,128)S(1)}, f32[128,128]{1,0:T(8,128)S(1)}) fusion(f32[64,128,128]{2,1,0:T(8,128)} %param.4, f32[]{:T(128)} %bitcast.10, f32[]{:T(128)} %bitcast.9, f32[]{:T(128)} %bitcast.8, f32[]{:T(128)} %bitcast.7, f32[]{:T(128)} %bitcast.20, f32[]{:T(128)} %bitcast.19, ...), kind=kOutput, calls=%fused_computation.28 | output fusion | flops 153026560 | bytes 9049196 | tf_op jit(solution)/shard_map/jit(cumsum)/reduce_window_sum | solution.py:38
  111.5 0.3 maximum_bitcast_fusion
  111.8 33.6 %all_to_all.18 = f32[1,4,128,128]{3,1,0,2:T(4,128)S(1)} all-to-all(f32[1,4,128,128]{3,1,0,2:T(4,128)S(1)} %maximum_bitcast_fusion), channel_id=1, replica_groups=mesh['ix'=4,'iy'=8,'depth'=16] {'depth'}, dimensions={2} | all-to-all | bytes 524288 | tf_op jit(solution)/shard_map/all_to_all | solution.py:54
  145.5 0.6 pad_maximum_fusion.11
  (8 shorter events, 0.2 us)
Async XLA Ops:
  0.9 7.4 %collective-permute-start = (f32[1,128,128]{2,1,0:T(8,128)S(1)}, f32[1,128,128]{2,1,0:T(8,128)S(1)}, u32[]{:S(2)}, u32[]{:S(2)}) collective-permute-start(f32[1,128,128]{2,1,0:T(8,128)S(1)} %get-tuple-element.14), channel_id=1, source_target_pairs={{0,1},{1,2},{2,3},{3,4},{4,5},{5,6},{6,7},{7,8},{8,9},{9,10},{10,1... | collective-permute-start | bytes 196616 | tf_op jit(solution)/shard_map/ppermute | solution.py:14
  5.3 5.8 %collective-permute-start.1 = (f32[1,128,128]{2,1,0:T(8,128)S(1)}, f32[1,128,128]{2,1,0:T(8,128)S(1)}, u32[]{:S(2)}, u32[]{:S(2)}) collective-permute-start(f32[1,128,128]{2,1,0:T(8,128)S(1)} %get-tuple-element.13), channel_id=1, source_target_pairs={{1,0},{2,1},{3,2},{4,3},{5,4},{6,5},{7,6},{8,7},{9,8},{10,9},{11,1... | collective-permute-start | bytes 196616 | tf_op jit(solution)/shard_map/ppermute | solution.py:15
  8.4 10.2 %copy-start.1 = (f32[4]{0:T(128)S(1)}, f32[4]{0:T(128)}, u32[]{:S(2)}) copy-start(f32[4]{0:T(128)} %param.6) | copy-start | bytes 52
  11.1 9.7 %copy-start = (f32[66,128,128]{2,1,0:T(8,128)}, f32[66,128,128]{2,1,0:T(8,128)S(1)}, u32[]{:S(2)}) copy-start(f32[66,128,128]{2,1,0:T(8,128)S(1)} %constant_dynamic-update-slice_fusion) | copy-start | bytes 12976132
  11.2 8.0 %collective-permute-start.2 = (f32[66,1,128]{2,1,0:T(1,128)S(1)}, f32[66,1,128]{2,1,0:T(1,128)S(1)}, u32[]{:S(2)}, u32[]{:S(2)}) collective-permute-start(f32[66,1,128]{2,1,0:T(1,128)S(1)} %get-tuple-element.12), channel_id=1, source_target_pairs={{0,16},{16,32},{32,48},{48,64},{64,80},{80,96},{96,112},{1,17},{17... | collective-permute-start | bytes 101384 | tf_op jit(solution)/shard_map/ppermute | solution.py:14
  15.5 5.2 %collective-permute-start.3 = (f32[66,1,128]{2,1,0:T(1,128)S(1)}, f32[66,1,128]{2,1,0:T(1,128)S(1)}, u32[]{:S(2)}, u32[]{:S(2)}) collective-permute-start(f32[66,1,128]{2,1,0:T(1,128)S(1)} %get-tuple-element.11), channel_id=1, source_target_pairs={{16,0},{32,16},{48,32},{64,48},{80,64},{96,80},{112,96},{17,1},{33... | collective-permute-start | bytes 101384 | tf_op jit(solution)/shard_map/ppermute | solution.py:15
  26.4 12.5 %copy-start.2 = (f32[3]{0:T(128)S(1)}, f32[3]{0:T(128)}, u32[]{:S(2)}) copy-start(f32[3]{0:T(128)} %param.7) | copy-start | bytes 40
  30.0 14.0 %collective-permute-start.4 = (f32[66,130,1]{0,2,1:T(1,128)S(1)}, f32[66,130,1]{0,2,1:T(1,128)S(1)}, u32[]{:S(2)}, u32[]{:S(2)}) collective-permute-start(f32[66,130,1]{0,2,1:T(1,128)S(1)} %copy.6), channel_id=1, source_target_pairs={{128,0},{256,128},{384,256},{129,1},{257,129},{385,257},{130,2},{2... | collective-permute-start | bytes 102968 | tf_op jit(solution)/shard_map/ppermute | solution.py:15
  34.9 12.5 %collective-permute-start.5 = (f32[66,130,1]{0,2,1:T(1,128)S(1)}, f32[66,130,1]{0,2,1:T(1,128)S(1)}, u32[]{:S(2)}, u32[]{:S(2)}) collective-permute-start(f32[66,130,1]{0,2,1:T(1,128)S(1)} %copy.8), channel_id=1, source_target_pairs={{0,128},{128,256},{256,384},{1,129},{129,257},{257,385},{2,130},{1... | collective-permute-start | bytes 102968 | tf_op jit(solution)/shard_map/ppermute | solution.py:14
where the time goes:
time: 147 us; the launch traced here: 146 us
  other arithmetic  62.4 us (42%)
  blocking collectives  33.6 us (23%)
  local copies, waits for them, and re-layouts  25.6 us (17%)
  starting transfers between devices  18.3 us (12%)
  between operations  4.61 us (3%)
  waiting for transfers between devices  1.63 us (1%)
    another operation x1, other arithmetic, shade_block(): before = jnp.cumsum(extinction, 0) - extinction  60.8 us
    all_to_all x1, blocking collectives, per_device(): lax.all_to_all(partial_value[None], 'depth', split_axis=2, concat_axis=0,...  33.6 us
    ppermute x3, starting transfers between devices, with_halo(): before = lax.ppermute(last, axis, up)  12.8 us
    slice x4, local copies, waits for them, and re-layouts, with_halo(): first = lax.slice_in_dim(x, 0, width, axis=dim)  9.46 us
    ppermute x3, starting transfers between devices, with_halo(): after = lax.ppermute(first, axis, down)  5.54 us
    slice x1, local copies, waits for them, and re-layouts, with_halo(): last = lax.slice_in_dim(x, length - width, length, axis=dim)  3.61 us
    ppermute x1, local copies, waits for them, and re-layouts, with_halo(): after = lax.ppermute(first, axis, down)  3.38 us
    ppermute x1, local copies, waits for them, and re-layouts, with_halo(): before = lax.ppermute(last, axis, up)  3.36 us
  transfers between devices with their start and end apart: 6, of which 1 were waited for; matrix products, arithmetic and copies ran while one was open for 9% of the time, Pallas kernels for 0%

commit v1 on v0

v1 whole, which is shorter than its diff:
```python
import functools
import math

import jax
import jax.numpy as jnp
from jax import lax
from jax.experimental import pallas as pl
from jax.experimental.pallas import tpu as pltpu
from jax.sharding import PartitionSpec as P

MESH = pl.DeviceIdType.MESH
LANES = 128
ROWS = 8
CHUNKS = 4
UNROLL = 8


def kernel(
    layers,
    density,
    color,
    opacity,
    light,
    image,
    brick,
    x_out,
    x_in,
    y_out,
    y_in,
    x_halo,
    sent,
    parts,
    color_s,
    opacity_s,
    light_s,
    load_sem,
    coeff_sem,
    halo_send,
    halo_recv,
    part_send,
    part_recv,
):
    brick_z, brick_y, _ = density.shape
    blocks = brick_y // ROWS
    ix, nx = lax.axis_index("ix"), lax.axis_size("ix")
    iy, ny = lax.axis_index("iy"), lax.axis_size("iy")
    me = lax.axis_index("depth")

    barrier = pltpu.get_barrier_semaphore()
    sides = (("ix", ix, nx), ("iy", iy, ny))

    def greet(step, carry):
        pl.semaphore_signal(
            barrier, inc=1, device_id={"depth": lax.rem(me + step, layers)}, device_id_type=MESH
        )
        return carry

    lax.fori_loop(1, layers, greet, 0)
    for axis, place, size in sides:

        @pl.when(place > 0)
        def _():
            pl.semaphore_signal(barrier, inc=1, device_id={axis: place - 1}, device_id_type=MESH)

        @pl.when(place < size - 1)
        def _():
            pl.semaphore_signal(barrier, inc=1, device_id={axis: place + 1}, device_id_type=MESH)

    span = brick_y // CHUNKS

    def load(chunk):
        return pltpu.make_async_copy(
            density.at[:, pl.ds(chunk * span, span), :],
            brick.at[pl.ds(1, brick_z), pl.ds(ROWS + chunk * span, span), :],
            load_sem.at[chunk],
        )

    for chunk in range(CHUNKS):
        load(chunk).start()
    coeffs = [
        pltpu.make_async_copy(source, target, coeff_sem.at[number])
        for number, (source, target) in enumerate(
            ((color, color_s), (opacity, opacity_s), (light, light_s))
        )
    ]
    for copy in coeffs:
        copy.start()

    lane = lax.broadcasted_iota(jnp.int32, (ROWS, LANES), 1)
    even = lax.rem(lane, 2) == 0
    pair = lane // 2
    per_chunk = blocks // CHUNKS

    def pack(chunk, carry):
        load(chunk).wait()
        base = pl.multiple_of(ROWS + chunk * span, ROWS)
        packed = [jnp.zeros((ROWS, LANES), jnp.float32) for _ in range(per_chunk)]
        for z in range(brick_z):
            here = pair == z
            for k in range(per_chunk):
                v = brick[z + 1, pl.ds(base + ROWS * k, ROWS), :]
                packed[k] = jnp.where(here, pltpu.roll(v, 2 * z + 1, 1), packed[k])
        half = pl.multiple_of(chunk * (span // 2), ROWS)
        for k in range(0, per_chunk, 2):
            a, b = packed[k], packed[k + 1]
            at = pl.ds(half + ROWS * (k // 2), ROWS)
            x_out[0, at, :] = jnp.where(even, pltpu.roll(a, LANES - 1, 1), b)
            x_out[1, at, :] = jnp.where(even, a, pltpu.roll(b, 1, 1))
        return carry

    lax.fori_loop(0, CHUNKS, pack, 0)
    y_out[0] = brick[pl.ds(1, brick_z), ROWS, :]
    y_out[1] = brick[pl.ds(1, brick_z), ROWS + brick_y - 1, :]

    greeted = layers - 1
    for _, place, size in sides:
        greeted = greeted + jnp.where(place > 0, 1, 0) + jnp.where(place < size - 1, 1, 0)
    pl.semaphore_wait(barrier, greeted)

    data = pl.ds(ROWS, brick_y)
    halos = []
    for number, (axis, place, size, down, up) in enumerate(
        (
            ("ix", ix, nx, (x_out.at[0], x_in.at[1]), (x_out.at[1], x_in.at[0])),
            ("iy", iy, ny, (y_out.at[0], y_in.at[1]), (y_out.at[1], y_in.at[0])),
            (
                "depth",
                me,
                layers,
                (density.at[0], brick.at[brick_z + 1, data, :]),
                (density.at[brick_z - 1], brick.at[0, data, :]),
            ),
        )
    ):
        lower, upper = place > 0, place < size - 1
        for way, (go, come, (source, target), step) in enumerate(
            ((lower, upper, down, -1), (upper, lower, up, 1))
        ):
            copy = pltpu.make_async_remote_copy(
                src_ref=source,
                dst_ref=target,
                send_sem=halo_send.at[2 * number + way],
                recv_sem=halo_recv.at[2 * number + way],
                device_id={axis: place + step},
                device_id_type=MESH,
            )
            halos.append((copy, go, come, target))
    for copy, go, come, target in halos:

        @pl.when(go)
        def _():
            copy.start()

        @pl.when(jnp.logical_not(come))
        def _():
            target[...] = jnp.zeros(target.shape, jnp.float32)

    for copy in coeffs:
        copy.wait()
    root = math.sqrt(3.0 / (brick_z * layers) * math.log2(math.e))
    o0, o1, o2, o3 = (opacity_s[k] * (root / 4.0**k) for k in range(4))
    lx, ly, lz = (0.7 * light_s[k] for k in range(3))
    squares = []
    for channel in range(3):
        c0, c1, c2, c3 = (color_s[channel, k] for k in range(4))
        squares.append(
            [
                c0 * c0,
                2.0 * c0 * c1 / 4.0,
                (2.0 * c0 * c2 + c1 * c1) / 16.0,
                2.0 * (c0 * c3 + c1 * c2) / 64.0,
                (2.0 * c1 * c3 + c2 * c2) / 256.0,
                2.0 * c2 * c3 / 1024.0,
                c3 * c3 / 4096.0,
            ]
        )

    for copy, go, come, target in halos:

        @pl.when(come)
        def _():
            copy.wait_recv()

    def unpack(k, carry):
        at = pl.ds(pl.multiple_of(ROWS * k, ROWS), ROWS)
        left, right = x_in[0, at, :], x_in[1, at, :]
        first = pl.multiple_of(2 * ROWS * k, ROWS)
        x_halo[pl.ds(first, ROWS), :] = jnp.where(even, left, pltpu.roll(right, 1, 1))
        x_halo[pl.ds(first + ROWS, ROWS), :] = jnp.where(
            even, pltpu.roll(left, LANES - 1, 1), right
        )
        return carry

    lax.fori_loop(0, blocks // 2, unpack, 0)
    brick[pl.ds(1, brick_z), ROWS - 1, :] = y_in[0]
    brick[pl.ds(1, brick_z), ROWS + brick_y, :] = y_in[1]

    is_first, is_last = lane == 0, lane == LANES - 1

    def part_copy(block):
        return pltpu.make_async_remote_copy(
            src_ref=sent.at[block],
            dst_ref=parts.at[me],
            send_sem=part_send.at[block],
            recv_sem=part_recv.at[me],
            device_id={"depth": block},
            device_id_type=MESH,
        )

    def cast(block):
        row = pl.multiple_of(ROWS * block, ROWS)
        halo = x_halo[pl.ds(row, ROWS), :]

        def cells(group, carry):
            total, before, moments = carry
            moments = list(moments)
            turned = pltpu.roll(halo, lax.rem(LANES - 2 * UNROLL * group, LANES), 1)
            for k in range(UNROLL):
                z = group * UNROLL + k
                v = brick[z + 1, pl.ds(row + ROWS, ROWS), :]
                edge = pltpu.roll(turned, LANES - (2 * k + 1), 1)
                gx = pltpu.roll(jnp.where(is_first, edge, v), LANES - 1, 1) - pltpu.roll(
                    jnp.where(is_last, edge, v), 1, 1
                )
                gy = (
                    brick[z + 1, pl.ds(row + ROWS + 1, ROWS), :]
                    - brick[z + 1, pl.ds(row + ROWS - 1, ROWS), :]
                )
                gz = (
                    brick[z + 2, pl.ds(row + ROWS, ROWS), :]
                    - brick[z, pl.ds(row + ROWS, ROWS), :]
                )
                facing = gx * lx + gy * ly + gz * lz
                norm = (gx * gx + gy * gy) + (gz * gz + 4.0)
                shading = jnp.abs(facing) * lax.rsqrt(norm) + 0.3
                p = ((o3 * v + o2) * v + o1) * v + o0
                total = total - p * p
                after = jnp.exp2(total)
                weight = (before - after) * shading
                before = after
                moments[0] = moments[0] + weight
                for degree in range(1, 7):
                    weight = weight * v
                    moments[degree] = moments[degree] + weight
            return total, before, tuple(moments)

        zero = jnp.zeros((ROWS, LANES), jnp.float32)
        _, clear, moments = lax.fori_loop(
            0, brick_z // UNROLL, cells, (zero, zero + 1.0, (zero,) * 7)
        )
        for channel in range(3):
            q = squares[channel]
            value = q[0] * moments[0]
            for degree in range(1, 7):
                value = value + q[degree] * moments[degree]
            sent[block, channel] = value
        sent[block, 3] = clear

    def others(step, carry):
        half = (step + 1) // 2
        hop = jnp.where(lax.rem(step, 2) == 0, layers // 2 + half, layers // 2 - half)
        block = lax.rem(me + hop, layers)
        cast(block)
        part_copy(block).start()
        return carry

    lax.fori_loop(0, layers - 1, others, 0)
    cast(me)

    def composite(layer, carry):
        red, green, blue, clear = carry

        @pl.when(layer != me)
        def _():
            pltpu.make_async_remote_copy(
                src_ref=sent.at[layer],
                dst_ref=parts.at[layer],
                send_sem=part_send.at[layer],
                recv_sem=part_recv.at[layer],
                device_id={"depth": layer},
                device_id_type=MESH,
            ).wait_recv()

        @pl.when(layer == me)
        def _():
            parts[layer] = sent[layer]

        return (
            red + clear * parts[layer, 0],
            green + clear * parts[layer, 1],
            blue + clear * parts[layer, 2],
            clear * parts[layer, 3],
        )

    zero = jnp.zeros((ROWS, LANES), jnp.float32)
    result = lax.fori_loop(0, layers, composite, (zero, zero, zero, zero + 1.0))
    for channel in range(4):
        image[channel] = result[channel]

    def finish(step, carry):
        part_copy(lax.rem(me + step, layers)).wait_send()
        return carry

    lax.fori_loop(1, layers, finish, 0)
    for copy, go, come, target in halos:

        @pl.when(go)
        def _():
            copy.wait_send()


def per_device(density, color_coeffs, opacity_coeffs, light):
    layers = lax.axis_size("depth")
    brick_z, brick_y, brick_x = density.shape
    blocks = brick_y // ROWS
    f32 = jnp.float32
    return pl.pallas_call(
        functools.partial(kernel, layers),
        out_shape=jax.ShapeDtypeStruct((4, ROWS, brick_x), f32),
        in_specs=[pl.BlockSpec(memory_space=pl.ANY)] * 4,
        out_specs=pl.BlockSpec(memory_space=pltpu.VMEM),
        scratch_shapes=[
            pltpu.VMEM((brick_z + 2, brick_y + 2 * ROWS, brick_x), f32),
            pltpu.VMEM((2, brick_y // 2, LANES), f32),
            pltpu.VMEM((2, brick_y // 2, LANES), f32),
            pltpu.VMEM((2, brick_z, LANES), f32),
            pltpu.VMEM((2, brick_z, LANES), f32),
            pltpu.VMEM((brick_y, LANES), f32),
            pltpu.VMEM((blocks, 4, ROWS, LANES), f32),
            pltpu.VMEM((layers, 4, ROWS, LANES), f32),
            pltpu.SMEM((3, 4), f32),
            pltpu.SMEM((4,), f32),
            pltpu.SMEM((3,), f32),
            pltpu.SemaphoreType.DMA((CHUNKS,)),
            pltpu.SemaphoreType.DMA((3,)),
            pltpu.SemaphoreType.DMA((6,)),
            pltpu.SemaphoreType.DMA((6,)),
            pltpu.SemaphoreType.DMA((blocks,)),
            pltpu.SemaphoreType.DMA((layers,)),
        ],
        compiler_params=pltpu.CompilerParams(
            collective_id=0, has_side_effects=True, vmem_limit_bytes=24 << 20
        ),
    )(density, color_coeffs, opacity_coeffs, light)


def solution(mesh):
    return jax.shard_map(
        per_device,
        mesh=mesh,
        in_specs=(P("depth", "iy", "ix"), P(), P(), P()),
        out_specs=P(None, ("iy", "depth"), "ix"),
        check_vma=False,
    )
```

time: 147 us -> 57.3 us (0.39)
  other arithmetic: 62.4 us -> 0 us
  Pallas kernels: 0 us -> 52.3 us
  blocking collectives: 33.6 us -> 0 us
  local copies, waits for them, and re-layouts: 25.6 us -> 4.79 us
  starting transfers between devices: 18.3 us -> 0 us
  between operations: 4.61 us -> 0.01 us
  waiting for transfers between devices: 1.63 us -> 0 us
    another operation x2 -> x0, other arithmetic: 60.8 us -> none  [the longest x1 60.8 us: shade_block(): before = jnp.cumsum(extinction, 0) - extinction]
    pallas_call x0 -> x1, Pallas kernels: none -> 52.3 us  [per_device(): pl.pallas_call(functools.partial(kernel, layers), out_shape=jax.ShapeDtyp...]
    all_to_all x1 -> x0, blocking collectives: 33.6 us -> none  [per_device(): lax.all_to_all(partial_value[None], 'depth', split_axis=2, concat_axis=0,...]
    ppermute x6 -> x0, starting transfers between devices: 18.3 us -> none  [the longest x3 12.8 us: with_halo(): before = lax.ppermute(last, axis, up)]
    slice x8 -> x0, local copies, waits for them, and re-layouts: 16.1 us -> none  [the longest x4 9.46 us: with_halo(): first = lax.slice_in_dim(x, 0, width, axis=dim)]
    ppermute x2 -> x0, local copies, waits for them, and re-layouts: 6.74 us -> none  [the longest x1 3.38 us: with_halo(): after = lax.ppermute(first, axis, down)]
    unnamed x8 -> x9, local copies, waits for them, and re-layouts: 2.71 us -> 4.79 us
    ppermute x6 -> x0, waiting for transfers between devices: 1.63 us -> none  [the longest x3 1.62 us: with_halo(): after = lax.ppermute(first, axis, down)]
  transfers between devices with their start and end apart: 6 -> 0, of which waited for: 1 -> 0; matrix products, arithmetic and copies ran while one was open for 9% -> 0% of each run, Pallas kernels for 0% -> 0%
where the time goes in v1:
time: 57.3 us; the launch traced here: 57.1 us
  Pallas kernels  52.3 us (91%)
  local copies, waits for them, and re-layouts  4.79 us (8%)
    pallas_call x1, Pallas kernels, per_device(): pl.pallas_call(functools.partial(kernel, layers), out_shape=jax.ShapeDtyp...  52.3 us
    unnamed x9, local copies, waits for them, and re-layouts  4.79 us

profile of v1, /device:TPU:1, one launch (start us, length us, event | category | flops | bytes accessed | tf_op | source)
XLA Modules:
  0.0 57.1 jit_solution(2064402518806846096)
XLA Ops:
  0.0 0.0 copy-start
  0.0 2.2 %copy-done = f32[64,128,128]{2,1,0:T(8,128)S(1)} copy-done((f32[64,128,128]{2,1,0:T(8,128)S(1)}, f32[64,128,128]{2,1,0:T(8,128)}, u32[]{:S(2)}) %copy-start) | copy-done | bytes 4194328
  2.2 0.0 copy-start.1
  2.2 0.7 %copy-done.1 = f32[3,4]{1,0:T(4,128)S(1)} copy-done((f32[3,4]{1,0:T(4,128)S(1)}, f32[3,4]{1,0:T(4,128)}, u32[]{:S(2)}) %copy-start.1) | copy-done | bytes 72
  2.9 0.0 copy-start.2
  2.9 0.7 %copy-done.2 = f32[4]{0:T(128)S(1)} copy-done((f32[4]{0:T(128)S(1)}, f32[4]{0:T(128)}, u32[]{:S(2)}) %copy-start.2) | copy-done | bytes 40
  3.5 0.0 copy-start.3
  3.5 0.7 %copy-done.3 = f32[3]{0:T(128)S(1)} copy-done((f32[3]{0:T(128)S(1)}, f32[3]{0:T(128)}, u32[]{:S(2)}) %copy-start.3) | copy-done | bytes 36
  4.2 52.3 %shard_map.46 = f32[4,8,128]{2,1,0:T(8,128)S(1)} custom-call(f32[64,128,128]{2,1,0:T(8,128)S(1)} %copy-done, f32[3,4]{1,0:T(4,128)S(1)} %copy-done.1, f32[4]{0:T(128)S(1)} %copy-done.2, f32[3]{0:T(128)S(1)} %copy-done.3), custom_call_target="tpu_custom_call" | custom-call | tf_op jit(solution)/shard_map/pallas_call | solution.py:317
  56.5 0.6 %copy.6 = f32[4,8,128]{2,1,0:T(8,128)} copy(f32[4,8,128]{2,1,0:T(8,128)S(1)} %shard_map.46) | data formatting | bytes 32768
Async XLA Ops:
  0.0 2.2 %copy-start = (f32[64,128,128]{2,1,0:T(8,128)S(1)}, f32[64,128,128]{2,1,0:T(8,128)}, u32[]{:S(2)}) copy-start(f32[64,128,128]{2,1,0:T(8,128)} %density.1) | copy-start | bytes 12582916
  2.2 0.7 %copy-start.1 = (f32[3,4]{1,0:T(4,128)S(1)}, f32[3,4]{1,0:T(4,128)}, u32[]{:S(2)}) copy-start(f32[3,4]{1,0:T(4,128)} %color.1) | copy-start | bytes 148
  2.9 0.7 %copy-start.2 = (f32[4]{0:T(128)S(1)}, f32[4]{0:T(128)}, u32[]{:S(2)}) copy-start(f32[4]{0:T(128)} %opacity.1) | copy-start | bytes 52
  3.5 0.7 %copy-start.3 = (f32[3]{0:T(128)S(1)}, f32[3]{0:T(128)}, u32[]{:S(2)}) copy-start(f32[3]{0:T(128)} %light.1) | copy-start | bytes 40

commit v2 on v1

--- a/solution.py
+++ b/solution.py
@@ -12,7 +12,6 @@
 LANES = 128
 ROWS = 8
 CHUNKS = 4
-UNROLL = 8
 
 
 def kernel(
@@ -211,43 +210,31 @@
         row = pl.multiple_of(ROWS * block, ROWS)
         halo = x_halo[pl.ds(row, ROWS), :]
 
-        def cells(group, carry):
-            total, before, moments = carry
-            moments = list(moments)
-            turned = pltpu.roll(halo, lax.rem(LANES - 2 * UNROLL * group, LANES), 1)
-            for k in range(UNROLL):
-                z = group * UNROLL + k
-                v = brick[z + 1, pl.ds(row + ROWS, ROWS), :]
-                edge = pltpu.roll(turned, LANES - (2 * k + 1), 1)
-                gx = pltpu.roll(jnp.where(is_first, edge, v), LANES - 1, 1) - pltpu.roll(
-                    jnp.where(is_last, edge, v), 1, 1
-                )
-                gy = (
-                    brick[z + 1, pl.ds(row + ROWS + 1, ROWS), :]
-                    - brick[z + 1, pl.ds(row + ROWS - 1, ROWS), :]
-                )
-                gz = (
-                    brick[z + 2, pl.ds(row + ROWS, ROWS), :]
-                    - brick[z, pl.ds(row + ROWS, ROWS), :]
-                )
-                facing = gx * lx + gy * ly + gz * lz
-                norm = (gx * gx + gy * gy) + (gz * gz + 4.0)
-                shading = jnp.abs(facing) * lax.rsqrt(norm) + 0.3
-                p = ((o3 * v + o2) * v + o1) * v + o0
-                total = total - p * p
-                after = jnp.exp2(total)
-                weight = (before - after) * shading
-                before = after
-                moments[0] = moments[0] + weight
-                for degree in range(1, 7):
-                    weight = weight * v
-                    moments[degree] = moments[degree] + weight
-            return total, before, tuple(moments)
-
         zero = jnp.zeros((ROWS, LANES), jnp.float32)
-        _, clear, moments = lax.fori_loop(
-            0, brick_z // UNROLL, cells, (zero, zero + 1.0, (zero,) * 7)
-        )
+        total, clear, moments = zero, zero + 1.0, [zero] * 7
+        for z in range(brick_z):
+            v = brick[z + 1, pl.ds(row + ROWS, ROWS), :]
+            edge = pltpu.roll(halo, LANES - (2 * z + 1), 1)
+            gx = pltpu.roll(jnp.where(is_first, edge, v), LANES - 1, 1) - pltpu.roll(
+                jnp.where(is_last, edge, v), 1, 1
+            )
+            gy = (
+                brick[z + 1, pl.ds(row + ROWS + 1, ROWS), :]
+                - brick[z + 1, pl.ds(row + ROWS - 1, ROWS), :]
+            )
+            gz = brick[z + 2, pl.ds(row + ROWS, ROWS), :] - brick[z, pl.ds(row + ROWS, ROWS), :]
+            facing = gx * lx + gy * ly + gz * lz
+            norm = (gx * gx + gy * gy) + (gz * gz + 4.0)
+            shading = jnp.abs(facing) * lax.rsqrt(norm) + 0.3
+            p = ((o3 * v + o2) * v + o1) * v + o0
+            total = total - p * p
+            after = jnp.exp2(total)
+            weight = (clear - after) * shading
+            clear = after
+            moments[0] = moments[0] + weight
+            for degree in range(1, 7):
+                weight = weight * v
+                moments[degree] = moments[degree] + weight
         for channel in range(3):
             q = squares[channel]
             value = q[0] * moments[0]
@@ -317,7 +304,7 @@
     return pl.pallas_call(
         functools.partial(kernel, layers),
         out_shape=jax.ShapeDtypeStruct((4, ROWS, brick_x), f32),
-        in_specs=[pl.BlockSpec(memory_space=pl.ANY)] * 4,
+        in_specs=[pl.BlockSpec(memory_space=pltpu.HBM)] * 4,
         out_specs=pl.BlockSpec(memory_space=pltpu.VMEM),
         scratch_shapes=[
             pltpu.VMEM((brick_z + 2, brick_y + 2 * ROWS, brick_x), f32),

time: 57.3 us -> 39.6 us (0.69)
  Pallas kernels: 52.3 us -> 34.6 us
    pallas_call x1, Pallas kernels: 52.3 us -> 34.6 us  [per_device(): pl.pallas_call(functools.partial(kernel, layers), out_shape=jax.ShapeDtyp...]
where the time goes in v2:
time: 39.6 us; the launch traced here: 39.4 us
  Pallas kernels  34.6 us (87%)
  local copies, waits for them, and re-layouts  4.79 us (12%)
    pallas_call x1, Pallas kernels, per_device(): pl.pallas_call(functools.partial(kernel, layers), out_shape=jax.ShapeDtyp...  34.6 us
    unnamed x9, local copies, waits for them, and re-layouts  4.79 us

profile of v2, /device:TPU:1, one launch (start us, length us, event | category | flops | bytes accessed | tf_op | source)
XLA Modules:
  0.0 39.4 jit_solution(17844485179076517974)
XLA Ops:
  0.0 0.0 copy-start
  0.0 2.2 %copy-done = f32[64,128,128]{2,1,0:T(8,128)S(1)} copy-done((f32[64,128,128]{2,1,0:T(8,128)S(1)}, f32[64,128,128]{2,1,0:T(8,128)}, u32[]{:S(2)}) %copy-start) | copy-done | bytes 4194328
  2.2 0.0 copy-start.1
  2.2 0.7 %copy-done.1 = f32[3,4]{1,0:T(4,128)S(1)} copy-done((f32[3,4]{1,0:T(4,128)S(1)}, f32[3,4]{1,0:T(4,128)}, u32[]{:S(2)}) %copy-start.1) | copy-done | bytes 72
  2.9 0.0 copy-start.2
  2.9 0.7 %copy-done.2 = f32[4]{0:T(128)S(1)} copy-done((f32[4]{0:T(128)S(1)}, f32[4]{0:T(128)}, u32[]{:S(2)}) %copy-start.2) | copy-done | bytes 40
  3.5 0.0 copy-start.3
  3.5 0.7 %copy-done.3 = f32[3]{0:T(128)S(1)} copy-done((f32[3]{0:T(128)S(1)}, f32[3]{0:T(128)}, u32[]{:S(2)}) %copy-start.3) | copy-done | bytes 36
  4.2 34.6 %shard_map.46 = f32[4,8,128]{2,1,0:T(8,128)S(1)} custom-call(f32[64,128,128]{2,1,0:T(8,128)S(1)} %copy-done, f32[3,4]{1,0:T(4,128)S(1)} %copy-done.1, f32[4]{0:T(128)S(1)} %copy-done.2, f32[3]{0:T(128)S(1)} %copy-done.3), custom_call_target="tpu_custom_call" | custom-call | tf_op jit(solution)/shard_map/pallas_call | solution.py:304
  38.8 0.6 %copy.6 = f32[4,8,128]{2,1,0:T(8,128)} copy(f32[4,8,128]{2,1,0:T(8,128)S(1)} %shard_map.46) | data formatting | bytes 32768
Async XLA Ops:
  0.0 2.2 %copy-start = (f32[64,128,128]{2,1,0:T(8,128)S(1)}, f32[64,128,128]{2,1,0:T(8,128)}, u32[]{:S(2)}) copy-start(f32[64,128,128]{2,1,0:T(8,128)} %density.1) | copy-start | bytes 12582916
  2.2 0.7 %copy-start.1 = (f32[3,4]{1,0:T(4,128)S(1)}, f32[3,4]{1,0:T(4,128)}, u32[]{:S(2)}) copy-start(f32[3,4]{1,0:T(4,128)} %color.1) | copy-start | bytes 148
  2.9 0.7 %copy-start.2 = (f32[4]{0:T(128)S(1)}, f32[4]{0:T(128)}, u32[]{:S(2)}) copy-start(f32[4]{0:T(128)} %opacity.1) | copy-start | bytes 52
  3.5 0.7 %copy-start.3 = (f32[3]{0:T(128)S(1)}, f32[3]{0:T(128)}, u32[]{:S(2)}) copy-start(f32[3]{0:T(128)} %light.1) | copy-start | bytes 40

commit v3 on v2

v3 whole, which is shorter than its diff:
```python
import functools
import math

import jax
import jax.numpy as jnp
from jax import lax
from jax.experimental import pallas as pl
from jax.experimental.pallas import tpu as pltpu
from jax.sharding import PartitionSpec as P

MESH = pl.DeviceIdType.MESH
LANES = 128
ROWS = 8
CHUNKS = 4


def kernel(
    layers,
    density,
    color,
    opacity,
    light,
    image,
    brick,
    opaque,
    x_out,
    x_in,
    y_out,
    y_in,
    x_halo,
    sent,
    parts,
    sent_clear,
    clears,
    color_s,
    opacity_s,
    light_s,
    load_sem,
    coeff_sem,
    halo_send,
    halo_recv,
    part_send,
    part_recv,
    clear_send,
    clear_recv,
):
    brick_z, brick_y, _ = density.shape
    blocks = brick_y // ROWS
    ix, nx = lax.axis_index("ix"), lax.axis_size("ix")
    iy, ny = lax.axis_index("iy"), lax.axis_size("iy")
    me = lax.axis_index("depth")

    barrier = pltpu.get_barrier_semaphore()
    sides = (("ix", ix, nx), ("iy", iy, ny))

    def greet(step, carry):
        pl.semaphore_signal(
            barrier, inc=1, device_id={"depth": lax.rem(me + step, layers)}, device_id_type=MESH
        )
        return carry

    lax.fori_loop(1, layers, greet, 0)
    for axis, place, size in sides:

        @pl.when(place > 0)
        def _():
            pl.semaphore_signal(barrier, inc=1, device_id={axis: place - 1}, device_id_type=MESH)

        @pl.when(place < size - 1)
        def _():
            pl.semaphore_signal(barrier, inc=1, device_id={axis: place + 1}, device_id_type=MESH)

    span = brick_y // CHUNKS

    def load(chunk):
        return pltpu.make_async_copy(
            density.at[:, pl.ds(chunk * span, span), :],
            brick.at[pl.ds(1, brick_z), pl.ds(ROWS + chunk * span, span), :],
            load_sem.at[chunk],
        )

    coeffs = [
        pltpu.make_async_copy(source, target, coeff_sem.at[number])
        for number, (source, target) in enumerate(
            ((opacity, opacity_s), (color, color_s), (light, light_s))
        )
    ]
    for copy in coeffs:
        copy.start()
    for chunk in range(CHUNKS):
        load(chunk).start()
    for copy in coeffs:
        copy.wait()
    root = math.sqrt(3.0 / (brick_z * layers) * math.log2(math.e))
    o0, o1, o2, o3 = (opacity_s[k] * (root / 4.0**k) for k in range(4))
    lx, ly, lz = (0.7 * light_s[k] for k in range(3))
    squares = []
    for channel in range(3):
        c0, c1, c2, c3 = (color_s[channel, k] for k in range(4))
        squares.append(
            [
                c0 * c0,
                2.0 * c0 * c1 / 4.0,
                (2.0 * c0 * c2 + c1 * c1) / 16.0,
                2.0 * (c0 * c3 + c1 * c2) / 64.0,
                (2.0 * c1 * c3 + c2 * c2) / 256.0,
                2.0 * c2 * c3 / 1024.0,
                c3 * c3 / 4096.0,
            ]
        )

    lane = lax.broadcasted_iota(jnp.int32, (ROWS, LANES), 1)
    even = lax.rem(lane, 2) == 0
    pair = lane // 2
    per_chunk = blocks // CHUNKS
    zero = jnp.zeros((ROWS, LANES), jnp.float32)

    def first_pass(chunk, carry):
        load(chunk).wait()
        base = pl.multiple_of(ROWS + chunk * span, ROWS)
        packed = [zero] * per_chunk
        for z in range(brick_z):
            here = pair == z
            for k in range(per_chunk):
                v = brick[z + 1, pl.ds(base + ROWS * k, ROWS), :]
                packed[k] = jnp.where(here, pltpu.roll(v, 2 * z + 1, 1), packed[k])
        half = pl.multiple_of(chunk * (span // 2), ROWS)
        for k in range(0, per_chunk, 2):
            a, b = packed[k], packed[k + 1]
            at = pl.ds(half + ROWS * (k // 2), ROWS)
            x_out[0, at, :] = jnp.where(even, pltpu.roll(a, LANES - 1, 1), b)
            x_out[1, at, :] = jnp.where(even, a, pltpu.roll(b, 1, 1))

        def hide(k, carry):
            row = pl.multiple_of(base + ROWS * k, ROWS)
            total, clear = zero, zero + 1.0
            for z in range(brick_z):
                v = brick[z + 1, pl.ds(row, ROWS), :]
                p = ((o3 * v + o2) * v + o1) * v + o0
                total = total - p * p
                after = jnp.exp2(total)
                opaque[z, pl.ds(row - ROWS, ROWS), :] = clear - after
                clear = after
            sent_clear[chunk * per_chunk + k] = clear
            return carry

        lax.fori_loop(0, per_chunk, hide, 0)
        return carry

    lax.fori_loop(0, CHUNKS, first_pass, 0)
    y_out[0] = brick[pl.ds(1, brick_z), ROWS, :]
    y_out[1] = brick[pl.ds(1, brick_z), ROWS + brick_y - 1, :]

    greeted = layers - 1
    for _, place, size in sides:
        greeted = greeted + jnp.where(place > 0, 1, 0) + jnp.where(place < size - 1, 1, 0)
    pl.semaphore_wait(barrier, greeted)

    data = pl.ds(ROWS, brick_y)
    halos = []
    for number, (axis, place, size, down, up) in enumerate(
        (
            (
                "depth",
                me,
                layers,
                (brick.at[1, data, :], brick.at[brick_z + 1, data, :]),
                (brick.at[brick_z, data, :], brick.at[0, data, :]),
            ),
            ("ix", ix, nx, (x_out.at[0], x_in.at[1]), (x_out.at[1], x_in.at[0])),
            ("iy", iy, ny, (y_out.at[0], y_in.at[1]), (y_out.at[1], y_in.at[0])),
        )
    ):
        lower, upper = place > 0, place < size - 1
        for way, (go, come, (source, target), step) in enumerate(
            ((lower, upper, down, -1), (upper, lower, up, 1))
        ):
            copy = pltpu.make_async_remote_copy(
                src_ref=source,
                dst_ref=target,
                send_sem=halo_send.at[2 * number + way],
                recv_sem=halo_recv.at[2 * number + way],
                device_id={axis: place + step},
                device_id_type=MESH,
            )
            halos.append((copy, go, come, target))
    for copy, go, come, target in halos:

        @pl.when(go)
        def _():
            copy.start()

        @pl.when(jnp.logical_not(come))
        def _():
            target[...] = jnp.zeros(target.shape, jnp.float32)

    def clear_copy(block, layer):
        return pltpu.make_async_remote_copy(
            src_ref=sent_clear.at[block],
            dst_ref=clears.at[layer],
            send_sem=clear_send.at[block],
            recv_sem=clear_recv.at[layer],
            device_id={"depth": block},
            device_id_type=MESH,
        )

    def part_copy(block, layer):
        return pltpu.make_async_remote_copy(
            src_ref=sent.at[block],
            dst_ref=parts.at[layer],
            send_sem=part_send.at[block],
            recv_sem=part_recv.at[layer],
            device_id={"depth": block},
            device_id_type=MESH,
        )

    half = layers // 2
    ahead = jnp.minimum(me, half)
    beyond = half - 1 - me

    def order(step):
        later = step - ahead
        swing = jnp.where(lax.rem(later, 2) == 0, half + later // 2, half - (later + 1) // 2)
        hop = jnp.where(later <= 2 * beyond, swing, half - (later - beyond))
        behind = half + lax.rem(later + me - half + 1, half)
        return jnp.where(step < ahead, step, jnp.where(me < half, me + hop, behind))

    def send_clear(step, carry):
        block = order(step)

        @pl.when(block != me)
        def _():
            clear_copy(block, me).start()

        return carry

    lax.fori_loop(0, blocks, send_clear, 0)

    for copy, go, come, target in halos:

        @pl.when(come)
        def _():
            copy.wait_recv()

    def unpack(k, carry):
        at = pl.ds(pl.multiple_of(ROWS * k, ROWS), ROWS)
        left, right = x_in[0, at, :], x_in[1, at, :]
        first = pl.multiple_of(2 * ROWS * k, ROWS)
        x_halo[pl.ds(first, ROWS), :] = jnp.where(even, left, pltpu.roll(right, 1, 1))
        x_halo[pl.ds(first + ROWS, ROWS), :] = jnp.where(
            even, pltpu.roll(left, LANES - 1, 1), right
        )
        return carry

    lax.fori_loop(0, blocks // 2, unpack, 0)
    brick[pl.ds(1, brick_z), ROWS - 1, :] = y_in[0]
    brick[pl.ds(1, brick_z), ROWS + brick_y, :] = y_in[1]

    is_first, is_last = lane == 0, lane == LANES - 1

    def shade(block):
        row = pl.multiple_of(ROWS * block, ROWS)
        halo = x_halo[pl.ds(row, ROWS), :]
        moments = [zero] * 7
        for z in range(brick_z):
            v = brick[z + 1, pl.ds(row + ROWS, ROWS), :]
            edge = pltpu.roll(halo, LANES - (2 * z + 1), 1)
            gx = pltpu.roll(jnp.where(is_first, edge, v), LANES - 1, 1) - pltpu.roll(
                jnp.where(is_last, edge, v), 1, 1
            )
            gy = (
                brick[z + 1, pl.ds(row + ROWS + 1, ROWS), :]
                - brick[z + 1, pl.ds(row + ROWS - 1, ROWS), :]
            )
            gz = brick[z + 2, pl.ds(row + ROWS, ROWS), :] - brick[z, pl.ds(row + ROWS, ROWS), :]
            facing = gx * lx + gy * ly + gz * lz
            norm = (gx * gx + gy * gy) + (gz * gz + 4.0)
            shading = jnp.abs(facing) * lax.rsqrt(norm) + 0.3
            weight = opaque[z, pl.ds(row, ROWS), :] * shading
            moments[0] = moments[0] + weight
            for degree in range(1, 7):
                weight = weight * v
                moments[degree] = moments[degree] + weight
        for channel in range(3):
            q = squares[channel]
            value = q[0] * moments[0]
            for degree in range(1, 7):
                value = value + q[degree] * moments[degree]
            sent[block, channel] = value

    def each(step, carry):
        block = order(step)
        shade(block)

        @pl.when(block != me)
        def _():
            part_copy(block, me).start()

        return carry

    lax.fori_loop(0, blocks, each, 0)

    def composite(layer, carry):
        red, green, blue, clear = carry

        @pl.when(layer != me)
        def _():
            clear_copy(layer, layer).wait_recv()
            part_copy(layer, layer).wait_recv()

        @pl.when(layer == me)
        def _():
            clears[layer] = sent_clear[layer]
            parts[layer] = sent[layer]

        return (
            red + clear * parts[layer, 0],
            green + clear * parts[layer, 1],
            blue + clear * parts[layer, 2],
            clear * clears[layer],
        )

    result = lax.fori_loop(0, layers, composite, (zero, zero, zero, zero + 1.0))
    for channel in range(4):
        image[channel] = result[channel]

    def finish(step, carry):
        block = lax.rem(me + step, layers)
        clear_copy(block, me).wait_send()
        part_copy(block, me).wait_send()
        return carry

    lax.fori_loop(1, layers, finish, 0)
    for copy, go, come, target in halos:

        @pl.when(go)
        def _():
            copy.wait_send()


def per_device(density, color_coeffs, opacity_coeffs, light):
    layers = lax.axis_size("depth")
    brick_z, brick_y, brick_x = density.shape
    blocks = brick_y // ROWS
    f32 = jnp.float32
    dma = pltpu.SemaphoreType.DMA
    return pl.pallas_call(
        functools.partial(kernel, layers),
        out_shape=jax.ShapeDtypeStruct((4, ROWS, brick_x), f32),
        in_specs=[pl.BlockSpec(memory_space=pltpu.HBM)] * 4,
        out_specs=pl.BlockSpec(memory_space=pltpu.VMEM),
        scratch_shapes=[
            pltpu.VMEM((brick_z + 2, brick_y + 2 * ROWS, brick_x), f32),
            pltpu.VMEM((brick_z, brick_y, brick_x), f32),
            pltpu.VMEM((2, brick_y // 2, LANES), f32),
            pltpu.VMEM((2, brick_y // 2, LANES), f32),
            pltpu.VMEM((2, brick_z, LANES), f32),
            pltpu.VMEM((2, brick_z, LANES), f32),
            pltpu.VMEM((brick_y, LANES), f32),
            pltpu.VMEM((blocks, 3, ROWS, LANES), f32),
            pltpu.VMEM((layers, 3, ROWS, LANES), f32),
            pltpu.VMEM((blocks, ROWS, LANES), f32),
            pltpu.VMEM((layers, ROWS, LANES), f32),
            pltpu.SMEM((3, 4), f32),
            pltpu.SMEM((4,), f32),
            pltpu.SMEM((3,), f32),
            dma((CHUNKS,)),
            dma((3,)),
            dma((6,)),
            dma((6,)),
            dma((blocks,)),
            dma((layers,)),
            dma((blocks,)),
            dma((layers,)),
        ],
        compiler_params=pltpu.CompilerParams(
            collective_id=0, has_side_effects=True, vmem_limit_bytes=60 << 20
        ),
    )(density, color_coeffs, opacity_coeffs, light)


def solution(mesh):
    return jax.shard_map(
        per_device,
        mesh=mesh,
        in_specs=(P("depth", "iy", "ix"), P(), P(), P()),
        out_specs=P(None, ("iy", "depth"), "ix"),
        check_vma=False,
    )
```

time: 39.6 us -> 33.5 us (0.85)
  the two profiles are of different devices: /device:TPU:1 before, /device:TPU:36 now
where the time goes in v3:
time: 33.5 us; the launch traced here: 33.4 us
  Pallas kernels  32 us (96%)
  local copies, waits for them, and re-layouts  1.32 us (4%)
    pallas_call x1, Pallas kernels, per_device(): pl.pallas_call(functools.partial(kernel, layers), out_shape=jax.ShapeDtyp...  32 us
    unnamed x1, local copies, waits for them, and re-layouts  1.32 us

profile of v3, /device:TPU:36, one launch (start us, length us, event | category | flops | bytes accessed | tf_op | source)
XLA Modules:
  0.0 33.4 jit_solution(10367779152300181058)
XLA Ops:
  0.0 32.0 %shard_map.46 = f32[4,8,128]{2,1,0:T(8,128)} custom-call(f32[64,128,128]{2,1,0:T(8,128)} %density.1, f32[3,4]{1,0:T(4,128)} %color.1, f32[4]{0:T(128)} %opacity.1, f32[3]{0:T(128)} %light.1), custom_call_target="tpu_custom_call" | custom-call | tf_op jit(solution)/shard_map/pallas_call | solution.py:347
  32.0 1.3 %copy.6 = f32[4,8,128]{2,1,0:T(8,128)} copy(f32[4,8,128]{2,1,0:T(8,128)} %shard_map.46) | data formatting | bytes 32768

commit v4 on v3

--- a/solution.py
+++ b/solution.py
@@ -53,13 +53,17 @@
     barrier = pltpu.get_barrier_semaphore()
     sides = (("ix", ix, nx), ("iy", iy, ny))
 
+    half = layers // 2
+
+    def swing(step):
+        return jnp.where(lax.rem(step, 2) == 0, half + step // 2, half - (step + 1) // 2)
+
     def greet(step, carry):
-        pl.semaphore_signal(
-            barrier, inc=1, device_id={"depth": lax.rem(me + step, layers)}, device_id_type=MESH
-        )
-        return carry
-
-    lax.fori_loop(1, layers, greet, 0)
+        other = lax.rem(me + swing(step), layers)
+        pl.semaphore_signal(barrier, inc=1, device_id={"depth": other}, device_id_type=MESH)
+        return carry
+
+    lax.fori_loop(0, layers - 1, greet, 0)
     for axis, place, size in sides:
 
         @pl.when(place > 0)
@@ -124,53 +128,58 @@
             for k in range(per_chunk):
                 v = brick[z + 1, pl.ds(base + ROWS * k, ROWS), :]
                 packed[k] = jnp.where(here, pltpu.roll(v, 2 * z + 1, 1), packed[k])
-        half = pl.multiple_of(chunk * (span // 2), ROWS)
+        first = pl.multiple_of(chunk * (span // 2), ROWS)
         for k in range(0, per_chunk, 2):
             a, b = packed[k], packed[k + 1]
-            at = pl.ds(half + ROWS * (k // 2), ROWS)
+            at = pl.ds(first + ROWS * (k // 2), ROWS)
             x_out[0, at, :] = jnp.where(even, pltpu.roll(a, LANES - 1, 1), b)
             x_out[1, at, :] = jnp.where(even, a, pltpu.roll(b, 1, 1))
-
-        def hide(k, carry):
-            row = pl.multiple_of(base + ROWS * k, ROWS)
-            total, clear = zero, zero + 1.0
-            for z in range(brick_z):
-                v = brick[z + 1, pl.ds(row, ROWS), :]
-                p = ((o3 * v + o2) * v + o1) * v + o0
-                total = total - p * p
-                after = jnp.exp2(total)
-                opaque[z, pl.ds(row - ROWS, ROWS), :] = clear - after
-                clear = after
-            sent_clear[chunk * per_chunk + k] = clear
-            return carry
-
-        lax.fori_loop(0, per_chunk, hide, 0)
+        return carry
+
+    def hide(block, carry):
+        row = pl.multiple_of(ROWS * block, ROWS)
+        total, clear = zero, zero + 1.0
+        for z in range(brick_z):
+            v = brick[z + 1, pl.ds(row + ROWS, ROWS), :]
+            p = ((o3 * v + o2) * v + o1) * v + o0
+            total = total - p * p
+            after = jnp.exp2(total)
+            opaque[z, pl.ds(row, ROWS), :] = clear - after
+            clear = after
+        sent_clear[block] = clear
         return carry
 
     lax.fori_loop(0, CHUNKS, first_pass, 0)
     y_out[0] = brick[pl.ds(1, brick_z), ROWS, :]
     y_out[1] = brick[pl.ds(1, brick_z), ROWS + brick_y - 1, :]
+
+    early = jnp.where(me < half, blocks, 4 * jnp.maximum(0, jnp.abs(me - half - 3) - 1))
+    lax.fori_loop(0, early, hide, 0)
 
     greeted = layers - 1
     for _, place, size in sides:
         greeted = greeted + jnp.where(place > 0, 1, 0) + jnp.where(place < size - 1, 1, 0)
     pl.semaphore_wait(barrier, greeted)
 
-    data = pl.ds(ROWS, brick_y)
+    def plane(chunk):
+        return pl.ds(ROWS + chunk * span, span)
+
+    lanes = [
+        (
+            "depth",
+            me,
+            layers,
+            (brick.at[1, plane(k), :], brick.at[brick_z + 1, plane(k), :]),
+            (brick.at[brick_z, plane(k), :], brick.at[0, plane(k), :]),
+        )
+        for k in range(CHUNKS)
+    ]
+    lanes[1:1] = [
+        ("ix", ix, nx, (x_out.at[0], x_in.at[1]), (x_out.at[1], x_in.at[0])),
+        ("iy", iy, ny, (y_out.at[0], y_in.at[1]), (y_out.at[1], y_in.at[0])),
+    ]
     halos = []
-    for number, (axis, place, size, down, up) in enumerate(
-        (
-            (
-                "depth",
-                me,
-                layers,
-                (brick.at[1, data, :], brick.at[brick_z + 1, data, :]),
-                (brick.at[brick_z, data, :], brick.at[0, data, :]),
-            ),
-            ("ix", ix, nx, (x_out.at[0], x_in.at[1]), (x_out.at[1], x_in.at[0])),
-            ("iy", iy, ny, (y_out.at[0], y_in.at[1]), (y_out.at[1], y_in.at[0])),
-        )
-    ):
+    for number, (axis, place, size, down, up) in enumerate(lanes):
         lower, upper = place > 0, place < size - 1
         for way, (go, come, (source, target), step) in enumerate(
             ((lower, upper, down, -1), (upper, lower, up, 1))
@@ -194,6 +203,8 @@
         def _():
             target[...] = jnp.zeros(target.shape, jnp.float32)
 
+    lax.fori_loop(early, blocks, hide, 0)
+
     def clear_copy(block, layer):
         return pltpu.make_async_remote_copy(
             src_ref=sent_clear.at[block],
@@ -214,14 +225,12 @@
             device_id_type=MESH,
         )
 
-    half = layers // 2
     ahead = jnp.minimum(me, half)
     beyond = half - 1 - me
 
     def order(step):
         later = step - ahead
-        swing = jnp.where(lax.rem(later, 2) == 0, half + later // 2, half - (later + 1) // 2)
-        hop = jnp.where(later <= 2 * beyond, swing, half - (later - beyond))
+        hop = jnp.where(later <= 2 * beyond, swing(later), half - (later - beyond))
         behind = half + lax.rem(later + me - half + 1, half)
         return jnp.where(step < ahead, step, jnp.where(me < half, me + hop, behind))
 
@@ -236,11 +245,14 @@
 
     lax.fori_loop(0, blocks, send_clear, 0)
 
-    for copy, go, come, target in halos:
-
-        @pl.when(come)
-        def _():
-            copy.wait_recv()
+    def arrive(some):
+        for copy, _, come, _ in some:
+
+            @pl.when(come)
+            def _():
+                copy.wait_recv()
+
+    arrive(halos[:6])
 
     def unpack(k, carry):
         at = pl.ds(pl.multiple_of(ROWS * k, ROWS), ROWS)
@@ -290,6 +302,15 @@
 
     def each(step, carry):
         block = order(step)
+
+        @pl.when(step == jnp.minimum(ahead, half // 2))
+        def _():
+            arrive(halos[6:8])
+
+        @pl.when(step == ahead)
+        def _():
+            arrive(halos[8:])
+
         shade(block)
 
         @pl.when(block != me)
@@ -338,7 +359,8 @@
             copy.wait_send()
 
 
-def per_device(density, color_coeffs, opacity_coeffs, light):
+def per_device(*arguments):
+    density = arguments[0]
     layers = lax.axis_size("depth")
     brick_z, brick_y, brick_x = density.shape
     blocks = brick_y // ROWS
@@ -366,17 +388,17 @@
             pltpu.SMEM((3,), f32),
             dma((CHUNKS,)),
             dma((3,)),
-            dma((6,)),
-            dma((6,)),
+            dma((2 * CHUNKS + 4,)),
+            dma((2 * CHUNKS + 4,)),
             dma((blocks,)),
             dma((layers,)),
             dma((blocks,)),
             dma((layers,)),
         ],
         compiler_params=pltpu.CompilerParams(
-            collective_id=0, has_side_effects=True, vmem_limit_bytes=60 << 20
+            collective_id=0, has_side_effects=True, vmem_limit_bytes=32 << 20
         ),
-    )(density, color_coeffs, opacity_coeffs, light)
+    )(*(pltpu.with_memory_space_constraint(a, pltpu.HBM) for a in arguments))
 
 
 def solution(mesh):

time: 33.5 us -> 32.1 us (0.958)
  the two profiles are of different devices: /device:TPU:36 before, /device:TPU:1 now
where the time goes in v4:
time: 32.1 us; the launch traced here: 32 us
  Pallas kernels  31.4 us (98%)
  local copies, waits for them, and re-layouts  0.61 us (2%)
    pallas_call x1, Pallas kernels, per_device(): pl.pallas_call(functools.partial(kernel, layers), out_shape=jax.ShapeDtyp...  31.4 us

profile of v4, /device:TPU:1, one launch (start us, length us, event | category | flops | bytes accessed | tf_op | source)
XLA Modules:
  0.0 32.0 jit_solution(10469122489812369586)
XLA Ops:
  0.0 31.4 %shard_map.46 = f32[4,8,128]{2,1,0:T(8,128)S(1)} custom-call(f32[64,128,128]{2,1,0:T(8,128)} %density.1, f32[3,4]{1,0:T(4,128)} %color.1, f32[4]{0:T(128)} %opacity.1, f32[3]{0:T(128)} %light.1), custom_call_target="tpu_custom_call" | custom-call | tf_op jit(solution)/shard_map/pallas_call | solution.py:369
  31.4 0.6 %copy.6 = f32[4,8,128]{2,1,0:T(8,128)} copy(f32[4,8,128]{2,1,0:T(8,128)S(1)} %shard_map.46) | data formatting | bytes 32768

commit v5 on v4

--- a/solution.py
+++ b/solution.py
@@ -12,6 +12,7 @@
 LANES = 128
 ROWS = 8
 CHUNKS = 4
+BETWEEN = 2
 
 
 def kernel(
@@ -23,6 +24,9 @@
     image,
     brick,
     opaque,
+    dots,
+    norms,
+    steps,
     x_out,
     x_in,
     y_out,
@@ -153,8 +157,30 @@
     y_out[0] = brick[pl.ds(1, brick_z), ROWS, :]
     y_out[1] = brick[pl.ds(1, brick_z), ROWS + brick_y - 1, :]
 
+    def slopes(block, z):
+        row = pl.multiple_of(ROWS * block, ROWS)
+        gy = (
+            brick[z + 1, pl.ds(row + ROWS + 1, ROWS), :]
+            - brick[z + 1, pl.ds(row + ROWS - 1, ROWS), :]
+        )
+        gz = brick[z + 2, pl.ds(row + ROWS, ROWS), :] - brick[z, pl.ds(row + ROWS, ROWS), :]
+        return gy * ly + gz * lz, gy * gy + (gz * gz + 4.0)
+
+    def across(block, z):
+        v = brick[z + 1, pl.ds(pl.multiple_of(ROWS * block + ROWS, ROWS), ROWS), :]
+        return pltpu.roll(v, LANES - 1, 1) - pltpu.roll(v, 1, 1)
+
+    def slope(block, carry=0):
+        at = pl.ds(pl.multiple_of(ROWS * block, ROWS), ROWS)
+        for z in range(1, brick_z - 1):
+            dots[z, at, :], norms[z, at, :] = slopes(block, z)
+            steps[z, at, :] = across(block, z)
+        return carry
+
     early = jnp.where(me < half, blocks, 4 * jnp.maximum(0, jnp.abs(me - half - 3) - 1))
     lax.fori_loop(0, early, hide, 0)
+    sloped = jnp.where(me < half, blocks - 1, 1)
+    lax.fori_loop(1, sloped, slope, 0)
 
     greeted = layers - 1
     for _, place, size in sides:
@@ -225,14 +251,18 @@
             device_id_type=MESH,
         )
 
-    ahead = jnp.minimum(me, half)
+    ahead = jnp.minimum(me, half // 2)
+    second = jnp.clip(me - half // 2, 0, half // 2)
     beyond = half - 1 - me
 
     def order(step):
-        later = step - ahead
+        place = step - ahead
+        later = place - jnp.where(place >= BETWEEN + second, second, 0)
         hop = jnp.where(later <= 2 * beyond, swing(later), half - (later - beyond))
         behind = half + lax.rem(later + me - half + 1, half)
-        return jnp.where(step < ahead, step, jnp.where(me < half, me + hop, behind))
+        rest = jnp.where(me < half, me + hop, behind)
+        inside = (place >= BETWEEN) & (place < BETWEEN + second)
+        return jnp.where(step < ahead, step, jnp.where(inside, half // 2 + place - BETWEEN, rest))
 
     def send_clear(step, carry):
         block = order(step)
@@ -252,43 +282,44 @@
             def _():
                 copy.wait_recv()
 
-    arrive(halos[:6])
+    lax.fori_loop(sloped, blocks - 1, slope, 0)
+    arrive(halos[4:6])
+    brick[pl.ds(1, brick_z), ROWS - 1, :] = y_in[0]
+    brick[pl.ds(1, brick_z), ROWS + brick_y, :] = y_in[1]
+    slope(0)
+    slope(blocks - 1)
+    arrive(halos[:4])
 
     def unpack(k, carry):
         at = pl.ds(pl.multiple_of(ROWS * k, ROWS), ROWS)
-        left, right = x_in[0, at, :], x_in[1, at, :]
-        first = pl.multiple_of(2 * ROWS * k, ROWS)
-        x_halo[pl.ds(first, ROWS), :] = jnp.where(even, left, pltpu.roll(right, 1, 1))
-        x_halo[pl.ds(first + ROWS, ROWS), :] = jnp.where(
-            even, pltpu.roll(left, LANES - 1, 1), right
+        last = x_in[1, at, :] - x_out[0, at, :]
+        first = x_out[1, at, :] - x_in[0, at, :]
+        row = pl.multiple_of(2 * ROWS * k, ROWS)
+        x_halo[pl.ds(row, ROWS), :] = jnp.where(even, last, pltpu.roll(first, 1, 1))
+        x_halo[pl.ds(row + ROWS, ROWS), :] = jnp.where(
+            even, pltpu.roll(last, LANES - 1, 1), first
         )
         return carry
 
     lax.fori_loop(0, blocks // 2, unpack, 0)
-    brick[pl.ds(1, brick_z), ROWS - 1, :] = y_in[0]
-    brick[pl.ds(1, brick_z), ROWS + brick_y, :] = y_in[1]
-
-    is_first, is_last = lane == 0, lane == LANES - 1
+    is_edge = (lane == 0) | (lane == LANES - 1)
 
     def shade(block):
         row = pl.multiple_of(ROWS * block, ROWS)
-        halo = x_halo[pl.ds(row, ROWS), :]
+        at = pl.ds(row, ROWS)
+        halo = x_halo[at, :]
         moments = [zero] * 7
         for z in range(brick_z):
             v = brick[z + 1, pl.ds(row + ROWS, ROWS), :]
             edge = pltpu.roll(halo, LANES - (2 * z + 1), 1)
-            gx = pltpu.roll(jnp.where(is_first, edge, v), LANES - 1, 1) - pltpu.roll(
-                jnp.where(is_last, edge, v), 1, 1
-            )
-            gy = (
-                brick[z + 1, pl.ds(row + ROWS + 1, ROWS), :]
-                - brick[z + 1, pl.ds(row + ROWS - 1, ROWS), :]
-            )
-            gz = brick[z + 2, pl.ds(row + ROWS, ROWS), :] - brick[z, pl.ds(row + ROWS, ROWS), :]
-            facing = gx * lx + gy * ly + gz * lz
-            norm = (gx * gx + gy * gy) + (gz * gz + 4.0)
-            shading = jnp.abs(facing) * lax.rsqrt(norm) + 0.3
-            weight = opaque[z, pl.ds(row, ROWS), :] * shading
+            if z in (0, brick_z - 1):
+                dot, norm = slopes(block, z)
+                gx = across(block, z)
+            else:
+                dot, norm, gx = dots[z, at, :], norms[z, at, :], steps[z, at, :]
+            gx = gx + jnp.where(is_edge, edge, 0.0)
+            shading = jnp.abs(gx * lx + dot) * lax.rsqrt(gx * gx + norm) + 0.3
+            weight = opaque[z, at, :] * shading
             moments[0] = moments[0] + weight
             for degree in range(1, 7):
                 weight = weight * v
@@ -303,13 +334,9 @@
     def each(step, carry):
         block = order(step)
 
-        @pl.when(step == jnp.minimum(ahead, half // 2))
-        def _():
-            arrive(halos[6:8])
-
         @pl.when(step == ahead)
         def _():
-            arrive(halos[8:])
+            arrive(halos[6:])
 
         shade(block)
 
@@ -373,7 +400,7 @@
         out_specs=pl.BlockSpec(memory_space=pltpu.VMEM),
         scratch_shapes=[
             pltpu.VMEM((brick_z + 2, brick_y + 2 * ROWS, brick_x), f32),
-            pltpu.VMEM((brick_z, brick_y, brick_x), f32),
+            *[pltpu.VMEM((brick_z, brick_y, brick_x), f32)] * 4,
             pltpu.VMEM((2, brick_y // 2, LANES), f32),
             pltpu.VMEM((2, brick_y // 2, LANES), f32),
             pltpu.VMEM((2, brick_z, LANES), f32),

time: 32.1 us -> 30.9 us (0.963)
  the two profiles are of different devices: /device:TPU:1 before, /device:TPU:56 now
where the time goes in v5:
time: 30.9 us; the launch traced here: 30.8 us
  Pallas kernels  30.1 us (97%)
  local copies, waits for them, and re-layouts  0.61 us (2%)
    pallas_call x1, Pallas kernels, per_device(): pl.pallas_call(functools.partial(kernel, layers), out_shape=jax.ShapeDtyp...  30.1 us

profile of v5, /device:TPU:56, one launch (start us, length us, event | category | flops | bytes accessed | tf_op | source)
XLA Modules:
  0.0 30.8 jit_solution(13962462473787618610)
XLA Ops:
  0.0 30.1 %shard_map.46 = f32[4,8,128]{2,1,0:T(8,128)S(1)} custom-call(f32[64,128,128]{2,1,0:T(8,128)} %density.1, f32[3,4]{1,0:T(4,128)} %color.1, f32[4]{0:T(128)} %opacity.1, f32[3]{0:T(128)} %light.1), custom_call_target="tpu_custom_call" | custom-call | tf_op jit(solution)/shard_map/pallas_call | solution.py:396
  30.2 0.6 %copy.6 = f32[4,8,128]{2,1,0:T(8,128)} copy(f32[4,8,128]{2,1,0:T(8,128)S(1)} %shard_map.46) | data formatting | bytes 32768

commit v6 on v5

--- a/solution.py
+++ b/solution.py
@@ -13,6 +13,7 @@
 ROWS = 8
 CHUNKS = 4
 BETWEEN = 2
+NEAR = 4
 
 
 def kernel(
@@ -47,6 +48,7 @@
     part_recv,
     clear_send,
     clear_recv,
+    open_sem,
 ):
     brick_z, brick_y, _ = density.shape
     blocks = brick_y // ROWS
@@ -62,9 +64,26 @@
     def swing(step):
         return jnp.where(lax.rem(step, 2) == 0, half + step // 2, half - (step + 1) // 2)
 
+    def excused(front, behind):
+        gap = behind - front
+        return (gap > NEAR) & (gap < layers - NEAR)
+
     def greet(step, carry):
         other = lax.rem(me + swing(step), layers)
-        pl.semaphore_signal(barrier, inc=1, device_id={"depth": other}, device_id_type=MESH)
+
+        @pl.when(jnp.logical_not(excused(other, me)))
+        def _():
+            pl.semaphore_signal(barrier, inc=1, device_id={"depth": other}, device_id_type=MESH)
+
+        return carry
+
+    def say(step, carry):
+        other = lax.rem(me + swing(step), layers)
+
+        @pl.when(excused(other, me))
+        def _():
+            pl.semaphore_signal(open_sem, inc=1, device_id={"depth": other}, device_id_type=MESH)
+
         return carry
 
     lax.fori_loop(0, layers - 1, greet, 0)
@@ -177,15 +196,10 @@
             steps[z, at, :] = across(block, z)
         return carry
 
-    early = jnp.where(me < half, blocks, 4 * jnp.maximum(0, jnp.abs(me - half - 3) - 1))
+    early = jnp.where(me < half, blocks, jnp.clip(half * (me - half - NEAR), 0, blocks))
     lax.fori_loop(0, early, hide, 0)
-    sloped = jnp.where(me < half, blocks - 1, 1)
+    sloped = jnp.where(me < half - 2, blocks - 1, 1)
     lax.fori_loop(1, sloped, slope, 0)
-
-    greeted = layers - 1
-    for _, place, size in sides:
-        greeted = greeted + jnp.where(place > 0, 1, 0) + jnp.where(place < size - 1, 1, 0)
-    pl.semaphore_wait(barrier, greeted)
 
     def plane(chunk):
         return pl.ds(ROWS + chunk * span, span)
@@ -219,17 +233,30 @@
                 device_id_type=MESH,
             )
             halos.append((copy, go, come, target))
-    for copy, go, come, target in halos:
-
-        @pl.when(go)
-        def _():
-            copy.start()
+    for _, _, come, target in halos:
 
         @pl.when(jnp.logical_not(come))
         def _():
             target[...] = jnp.zeros(target.shape, jnp.float32)
 
+    some_excused = me <= layers - 2 - NEAR
+    missing = jnp.clip(layers - 1 - NEAR - me, 0, layers - 1 - 2 * NEAR)
+    greeted = layers - 1 - missing
+    for _, place, size in sides:
+        greeted = greeted + jnp.where(place > 0, 1, 0) + jnp.where(place < size - 1, 1, 0)
+    pl.semaphore_wait(barrier, greeted)
+
+    def leave(some):
+        for copy, go, _, _ in some:
+
+            @pl.when(go)
+            def _():
+                copy.start()
+
+    leave(halos[:6])
     lax.fori_loop(early, blocks, hide, 0)
+    leave(halos[6:])
+    lax.fori_loop(0, layers - 1, say, 0)
 
     def clear_copy(block, layer):
         return pltpu.make_async_remote_copy(
@@ -253,21 +280,38 @@
 
     ahead = jnp.minimum(me, half // 2)
     second = jnp.clip(me - half // 2, 0, half // 2)
-    beyond = half - 1 - me
+
+    behind_near = jnp.minimum(NEAR, layers - 1 - me)
+
+    def centre(step):
+        near = step - ahead
+        front = near - behind_near
+        return jnp.where(
+            step < ahead,
+            step,
+            jnp.where(
+                near < behind_near,
+                me + behind_near - near,
+                jnp.where(
+                    front < me - ahead,
+                    ahead + front,
+                    jnp.where(front == me - ahead, me, layers - 1 - (step - me - behind_near - 1)),
+                ),
+            ),
+        )
 
     def order(step):
         place = step - ahead
         later = place - jnp.where(place >= BETWEEN + second, second, 0)
-        hop = jnp.where(later <= 2 * beyond, swing(later), half - (later - beyond))
-        behind = half + lax.rem(later + me - half + 1, half)
-        rest = jnp.where(me < half, me + hop, behind)
+        rest = half + lax.rem(later + me - half + 1, half)
         inside = (place >= BETWEEN) & (place < BETWEEN + second)
-        return jnp.where(step < ahead, step, jnp.where(inside, half // 2 + place - BETWEEN, rest))
+        usual = jnp.where(step < ahead, step, jnp.where(inside, half // 2 + place - BETWEEN, rest))
+        return jnp.where(some_excused, centre(step), usual)
 
     def send_clear(step, carry):
         block = order(step)
 
-        @pl.when(block != me)
+        @pl.when((block != me) & jnp.logical_not(excused(me, block)))
         def _():
             clear_copy(block, me).start()
 
@@ -301,7 +345,7 @@
         )
         return carry
 
-    lax.fori_loop(0, blocks // 2, unpack, 0)
+    lax.fori_loop(0, per_chunk // 2, unpack, 0)
     is_edge = (lane == 0) | (lane == LANES - 1)
 
     def shade(block):
@@ -337,40 +381,30 @@
         @pl.when(step == ahead)
         def _():
             arrive(halos[6:])
+            lax.fori_loop(per_chunk // 2, blocks // 2, unpack, 0)
 
         shade(block)
 
-        @pl.when(block != me)
+        @pl.when((block != me) & jnp.logical_not(excused(me, block)))
         def _():
             part_copy(block, me).start()
 
         return carry
 
-    lax.fori_loop(0, blocks, each, 0)
-
-    def composite(layer, carry):
-        red, green, blue, clear = carry
-
-        @pl.when(layer != me)
-        def _():
-            clear_copy(layer, layer).wait_recv()
-            part_copy(layer, layer).wait_recv()
-
-        @pl.when(layer == me)
-        def _():
-            clears[layer] = sent_clear[layer]
-            parts[layer] = sent[layer]
-
-        return (
-            red + clear * parts[layer, 0],
-            green + clear * parts[layer, 1],
-            blue + clear * parts[layer, 2],
-            clear * clears[layer],
-        )
-
-    result = lax.fori_loop(0, layers, composite, (zero, zero, zero, zero + 1.0))
-    for channel in range(4):
-        image[channel] = result[channel]
+    lax.fori_loop(0, blocks - missing, each, 0)
+
+    @pl.when(missing > 0)
+    def _():
+        pl.semaphore_wait(open_sem, missing)
+
+    def each_excused(step, carry):
+        block = order(step)
+        clear_copy(block, me).start()
+        shade(block)
+        part_copy(block, me).start()
+        return carry
+
+    lax.fori_loop(blocks - missing, blocks, each_excused, 0)
 
     def finish(step, carry):
         block = lax.rem(me + step, layers)
@@ -379,11 +413,28 @@
         return carry
 
     lax.fori_loop(1, layers, finish, 0)
-    for copy, go, come, target in halos:
+    for copy, go, _, _ in halos:
 
         @pl.when(go)
         def _():
             copy.wait_send()
+
+    clears[me] = sent_clear[me]
+    parts[me] = sent[me]
+
+    def gather(step, carry):
+        layer = lax.rem(me + swing(layers - 2 - step), layers)
+        clear_copy(layer, layer).wait_recv()
+        part_copy(layer, layer).wait_recv()
+        return carry
+
+    lax.fori_loop(0, layers - 1, gather, 0)
+    result, clear = [zero] * 3, zero + 1.0
+    for layer in range(layers):
+        result = [value + clear * parts[layer, k] for k, value in enumerate(result)]
+        clear = clear * clears[layer]
+    for channel, value in enumerate([*result, clear]):
+        image[channel] = value
 
 
 def per_device(*arguments):
@@ -421,6 +472,7 @@
             dma((layers,)),
             dma((blocks,)),
             dma((layers,)),
+            pltpu.SemaphoreType.REGULAR,
         ],
         compiler_params=pltpu.CompilerParams(
             collective_id=0, has_side_effects=True, vmem_limit_bytes=32 << 20

time: 30.9 us -> 29.2 us (0.945)
  the two profiles are of different devices: /device:TPU:56 before, /device:TPU:116 now
where the time goes in v6:
time: 29.2 us; the launch traced here: 29.1 us
  Pallas kernels  28.4 us (97%)
  local copies, waits for them, and re-layouts  0.61 us (2%)
    pallas_call x1, Pallas kernels, per_device(): pl.pallas_call(functools.partial(kernel, layers), out_shape=jax.ShapeDtyp...  28.4 us
    unnamed x1, local copies, waits for them, and re-layouts  0.61 us

profile of v6, /device:TPU:116, one launch (start us, length us, event | category | flops | bytes accessed | tf_op | source)
XLA Modules:
  0.0 29.1 jit_solution(9005642073904566367)
XLA Ops:
  0.0 28.4 %shard_map.46 = f32[4,8,128]{2,1,0:T(8,128)S(1)} custom-call(f32[64,128,128]{2,1,0:T(8,128)} %density.1, f32[3,4]{1,0:T(4,128)} %color.1, f32[4]{0:T(128)} %opacity.1, f32[3]{0:T(128)} %light.1), custom_call_target="tpu_custom_call" | custom-call | tf_op jit(solution)/shard_map/pallas_call | solution.py:447
  28.4 0.6 %copy.6 = f32[4,8,128]{2,1,0:T(8,128)} copy(f32[4,8,128]{2,1,0:T(8,128)S(1)} %shard_map.46) | data formatting | bytes 32768

commit v7 on v6

--- a/solution.py
+++ b/solution.py
@@ -300,7 +300,11 @@
             ),
         )
 
+    yields = (me >= half // 2) & (lax.rem(iy, 2) == 1)
+
     def order(step):
+        held = yields & (step >= 2) & (step < 6)
+        step = jnp.where(held, 2 + lax.rem(step, 4), step)
         place = step - ahead
         later = place - jnp.where(place >= BETWEEN + second, second, 0)
         rest = half + lax.rem(later + me - half + 1, half)
@@ -378,7 +382,7 @@
     def each(step, carry):
         block = order(step)
 
-        @pl.when(step == ahead)
+        @pl.when(step == jnp.where(yields, 2, ahead))
         def _():
             arrive(halos[6:])
             lax.fori_loop(per_chunk // 2, blocks // 2, unpack, 0)

time: 29.2 us -> 28.9 us (0.990)
  the two profiles are of different devices: /device:TPU:116 before, /device:TPU:158 now
where the time goes in v7:
time: 28.9 us; the launch traced here: 28.8 us
  Pallas kernels  28.2 us (98%)
  local copies, waits for them, and re-layouts  0.61 us (2%)
    pallas_call x1, Pallas kernels, per_device(): pl.pallas_call(functools.partial(kernel, layers), out_shape=jax.ShapeDtyp...  28.2 us
    unnamed x1, local copies, waits for them, and re-layouts  0.61 us

profile of v7, /device:TPU:158, one launch (start us, length us, event | category | flops | bytes accessed | tf_op | source)
XLA Modules:
  0.0 28.8 jit_solution(746298822845177928)
XLA Ops:
  0.0 28.2 %shard_map.46 = f32[4,8,128]{2,1,0:T(8,128)S(1)} custom-call(f32[64,128,128]{2,1,0:T(8,128)} %density.1, f32[3,4]{1,0:T(4,128)} %color.1, f32[4]{0:T(128)} %opacity.1, f32[3]{0:T(128)} %light.1), custom_call_target="tpu_custom_call" | custom-call | tf_op jit(solution)/shard_map/pallas_call | solution.py:451
  28.2 0.6 %copy.6 = f32[4,8,128]{2,1,0:T(8,128)} copy(f32[4,8,128]{2,1,0:T(8,128)S(1)} %shard_map.46) | data formatting | bytes 32768
